TPU v7x, 32 devices: a whole 2x2x4 slice. The times are simulated.
32 devices in a mesh: vc: 4 (over z), vd: 8 (over y, x, core).
Axes of the slice: x: 2, y: 2, z: 4, core: 2. Of those that a mesh axis runs over, the one named last changes fastest.
Arguments:
- vectors_left: float32 [8, 1024, 4096], P(None, 'vc', 'vd'), may hold values from -0.8 to 0.8
- vectors_right: float32 [16, 1024, 4096], P(None, 'vd', 'vc'), may hold values from -0.8 to 0.8
- amplitudes: float32 [1024, 1024, 128], P('vc', 'vd'), may hold values from -0.005859375 to 0.005859375
Outputs:
- ladder: float32 [128, 8, 16], P('vd', None, 'vc')
All inputs are finite; a program needn't handle non-finite values.
Results may differ from a plain program's by a relative error of at most 0.000094.
Values sent between devices are 32-bit elements; how exact they have to be, the bound alone decides.
A program may use at most 192 MiB of HBM per device.

v0:
```python
import jax
import jax.numpy as jnp
from jax import lax
from jax.sharding import PartitionSpec as P


def contract(left_rows, right_rows):
    return lax.dot_general(
        left_rows,
        right_rows,
        (((1,), (1,)), ((), ())),
        precision=lax.Precision.HIGHEST,
        preferred_element_type=jnp.float32,
    )


def shards(vectors_left, vectors_right, amplitudes):
    count_a, count_c, left_q = vectors_left.shape
    count_b, count_d, right_q = vectors_right.shape
    left_whole = lax.all_gather(vectors_left, "vd", axis=2, tiled=True)
    left_flat = left_whole.reshape(count_a * count_c, left_whole.shape[2])
    piece = lax.all_gather(vectors_right, "vc", axis=2, tiled=True)
    width = piece.shape[2]
    tile = contract(left_flat, piece.reshape(count_b * count_d, width))
    tile = tile.reshape(count_a, count_c, count_b, count_d)
    partial_sum = jnp.einsum("acbd,cdi->iab", tile, amplitudes, precision=lax.Precision.HIGHEST)
    reduced = lax.psum_scatter(partial_sum, "vd", scatter_dimension=0, tiled=True)
    ladder = lax.psum_scatter(reduced, "vc", scatter_dimension=2, tiled=True)
    return ladder


def solution(mesh):
    return jax.shard_map(
        shards,
        mesh=mesh,
        in_specs=(P(None, "vc", "vd"), P(None, "vd", "vc"), P("vc", "vd", None)),
        out_specs=P("vd", None, "vc"),
        check_vma=False,
    )
```

profile of v0, /device:TPU:0, one launch (start us, length us, event | category | flops | bytes accessed | tf_op | source)
XLA Modules:
  0.0 1053.6 jit_solution(2353245740148917430)
XLA Ops:
  6.5 0.0 all-gather.5.cloned.1.call-start
  6.5 0.7 all-gather.5.cloned.1.call-update
  7.3 0.0 all-gather.3.cloned.1.call-start
  7.3 0.7 all-gather.3.cloned.1.call-update
  8.0 0.0 reduce-scatter.7.cloned.1.call-start
  8.1 565.0 %all-gather.5.cloned.1.call-done = f32[16,128,4096]{2,1,0:T(8,128)} async-done(((f32[16,128,1024]{2,1,0:T(8,128)}), f32[16,128,4096]{2,1,0:T(8,128)}) %all-gather.5.cloned.1.call-update) | async-done | bytes 33554448 | tf_op jit(solution)/shard_map/all_gather | solution.py:22
  573.1 160.9 %all-gather.3.cloned.1.call-done = f32[8,256,4096]{2,1,0:T(8,128)} async-done(((f32[8,256,512]{2,1,0:T(8,128)}), f32[8,256,4096]{2,1,0:T(8,128)}) %all-gather.3.cloned.1.call-update) | async-done | bytes 33554448 | tf_op jit(solution)/shard_map/all_gather | solution.py:20
  734.0 221.6 %fusion = f32[8,256,16,128]{3,1,2,0:T(8,128)} fusion(f32[8,256,4096]{2,1,0:T(8,128)} %all-gather.3.cloned.1.call-done, f32[16,128,4096]{2,1,0:T(8,128)} %all-gather.5.cloned.1.call-done), kind=kOutput, calls=%fused_computation | convolution fusion | flops 206158430208 | bytes 83886080 | tf_op jit(solution)/shard_map/dot_general | solution.py:8
  955.6 34.8 %fusion.3 = f32[8,16,128,1]{2,1,3,0:T(8,128)S(1)} fusion(f32[256,128,128]{2,1,0:T(8,128)} %param.5, f32[8,256,16,128]{3,1,2,0:T(8,128)} %fusion), kind=kOutput, calls=%fused_computation.3 | convolution fusion | flops 6442450944 | bytes 33619968 | tf_op jit(solution)/shard_map/acbd,cdi->iab/dot_general | solution.py:26
  990.4 0.7 copy.11
  991.1 0.0 reduce-scatter.7.cloned.1.call-update
  991.1 0.0 reduce-scatter.5.cloned.1.call-start
  991.2 33.3 %reduce-scatter.7.cloned.1.call-done = f32[16,128]{1,0:T(8,128)} async-done(((f32[128,128]{1,0:T(8,128)}), f32[16,128]{1,0:T(8,128)}) %reduce-scatter.7.cloned.1.call-update) | async-done | bytes 8208
  1024.5 0.8 copy.12
  1025.3 0.7 copy.4
  1026.0 0.0 reduce-scatter.5.cloned.1.call-update
  1026.0 19.8 %reduce-scatter.5.cloned.1.call-done = f32[16,8,4]{0,1,2:T(8,128)} async-done(((f32[16,8,16]{0,1,2:T(8,128)}), f32[16,8,4]{0,1,2:T(8,128)}) %reduce-scatter.5.cloned.1.call-update) | async-done | bytes 2064 | tf_op jit(solution)/shard_map/reduce_scatter | solution.py:28
  1045.8 1.3 copy.5
Async XLA Ops:
  6.5 566.5 %all-gather.5.cloned.1.call-start = ((), (), s32[]{:S(2)}) async-start(), calls=%async_computation.3 | async-start | bytes 41943040 | tf_op jit(solution)/shard_map/all_gather | solution.py:22
  7.3 726.7 %all-gather.3.cloned.1.call-start = ((), (), s32[]{:S(2)}) async-start(), calls=%async_computation.2 | async-start | bytes 37748736 | tf_op jit(solution)/shard_map/all_gather | solution.py:20
  8.0 1016.5 %reduce-scatter.7.cloned.1.call-start = ((), (), s32[]{:S(2)}) async-start(), calls=%async_computation.5 | async-start | bytes 73728
  991.1 54.6 %reduce-scatter.5.cloned.1.call-start = ((), (), s32[]{:S(2)}) async-start(), calls=%async_computation.4 | async-start | bytes 81920 | tf_op jit(solution)/shard_map/reduce_scatter | solution.py:28
Sparse Core Ops, SparseCore 0:
  8.9 564.0 all-gather.4
  575.0 158.9 all-gather.2
  991.3 33.2 reduce-scatter.6
  1026.7 19.0 reduce-scatter.4
where the time goes:
time: 1050 us
  waiting for transfers between devices  780 us (74%)
  matrix products  256 us (24%)
  between operations  13.1 us (1%)
    all_gather x1, waiting for transfers between devices, shards(): piece = lax.all_gather(vectors_right, 'vc', axis=2, tiled=True)  565 us
    dot_general x1, matrix products, contract(): lax.dot_general(left_rows, right_rows, (((1,), (1,)), ((), ())), precisio...  222 us
    all_gather x1, waiting for transfers between devices, shards(): left_whole = lax.all_gather(vectors_left, 'vd', axis=2, tiled=True)  161 us
    dot_general x1, matrix products, shards(): jnp.einsum('acbd,cdi->iab', tile, amplitudes, precision=lax.Precision.HIG...  34.8 us
    unnamed x5, waiting for transfers between devices  34.8 us
  transfers between devices with their start and end apart: 4, of which 4 were waited for; matrix products, arithmetic and copies ran while one was open for 0% of the time, Pallas kernels for 0%

commit v1 on v0

v1 whole, which is shorter than its diff:
```python
import functools

import jax
import jax.numpy as jnp
from jax import lax
from jax.experimental import pallas as pl
from jax.experimental.pallas import tpu as pltpu
from jax.sharding import PartitionSpec as P

MESH = pl.DeviceIdType.MESH
CHUNK = 256
AHEAD = 2


def contract(left_rows, right_rows):
    return lax.dot_general(
        left_rows,
        right_rows,
        (((1,), (1,)), ((), ())),
        precision=lax.Precision.HIGHEST,
        preferred_element_type=jnp.float32,
    )


def plain(vectors_left, vectors_right, amplitudes):
    count_a, count_c, left_q = vectors_left.shape
    count_b, count_d, right_q = vectors_right.shape
    left_whole = lax.all_gather(vectors_left, "vd", axis=2, tiled=True)
    left_flat = left_whole.reshape(count_a * count_c, left_whole.shape[2])
    piece = lax.all_gather(vectors_right, "vc", axis=2, tiled=True)
    width = piece.shape[2]
    tile = contract(left_flat, piece.reshape(count_b * count_d, width))
    tile = tile.reshape(count_a, count_c, count_b, count_d)
    partial_sum = jnp.einsum("acbd,cdi->iab", tile, amplitudes, precision=lax.Precision.HIGHEST)
    reduced = lax.psum_scatter(partial_sum, "vd", scatter_dimension=0, tiled=True)
    return lax.psum_scatter(reduced, "vc", scatter_dimension=2, tiled=True)


def split(x):
    hi = x.astype(jnp.bfloat16)
    lo = (x - hi.astype(jnp.float32)).astype(jnp.bfloat16)
    return hi, lo


def kernel(nz, nd, main, left, right, amps, out, lg, rg, te, acc, own_rest, far_rest,
           lbuf, rbuf, ls, rs, tbuf, total, red_d, red_c,
           z_send, z_recv, m_send, m_recv, e_send, e_recv, le_send, le_recv, te_send, te_recv,
           lg_send, lg_recv, d_send, d_recv, c_send, c_recv, local, tsem):
    count_a, count_c, left_q = left.shape
    count_d, count_b, right_q = right.shape
    rest = count_d - main
    per = right_q // CHUNK
    half = left_q // 2
    rows_main, rows_rest = main * count_b, rest * count_b
    i = lax.axis_index("vc")
    j = lax.axis_index("vd")
    core, x, y = j % 2, (j // 2) % 2, j // 4
    jx, jy, js = j + 2 - 4 * x, j + 4 - 8 * y, j + 1 - 2 * core
    jd = jx + 4 - 8 * y
    is_end = (i == 0) | (i == nz - 1)
    middle = jnp.logical_not(is_end)
    low = i < nz // 2
    partner = jnp.where(low, 1 - i, 2 * nz - 3 - i)
    across = nz - 1 - i

    barrier = pltpu.get_barrier_semaphore()
    for step in range(1, nd):
        pl.semaphore_signal(barrier, inc=1, device_id=(i, (j + step) % nd), device_id_type=MESH)
    for step in range(1, nz):
        pl.semaphore_signal(barrier, inc=1, device_id=((i + step) % nz, j), device_id_type=MESH)
    pl.semaphore_wait(barrier, nd - 1 + nz - 1)

    def remote(src, dst, send, recv, who):
        return pltpu.make_async_remote_copy(
            src_ref=src, dst_ref=dst, send_sem=send, recv_sem=recv, device_id=who, device_id_type=MESH)

    n_send = (jnp.where(i < nz - 1, per * (i + 1), 0), jnp.where(i > 0, per * (nz - i), 0))
    n_recv = (per * i, per * (nz - 1 - i))

    def z_copy(way, n, src_own):
        block = jnp.where(way == 0, i - n // per, i + n // per) if src_own is None else i
        cols = pl.ds(pl.multiple_of((n % per) * CHUNK, CHUNK), CHUNK)
        dst = rg.at[block, pl.ds(0, main), :, cols]
        src = right.at[pl.ds(0, main), :, cols] if src_own else dst
        who = (i + 1, j) if way == 0 else (i - 1, j)
        return remote(src, dst, z_send.at[way, n], z_recv.at[way, n], who)

    def z_start(way, n):
        @pl.when((n < per) & (n < n_send[way]))
        def _():
            z_copy(way, n, True).start()

        @pl.when((n >= per) & (n < n_send[way]))
        def _():
            z_copy(way, n, None).start()

    def z_wait_recv(way, n):
        block = i - 1 - n // per if way == 0 else i + 1 + n // per
        cols = pl.ds(pl.multiple_of((n % per) * CHUNK, CHUNK), CHUNK)
        dst = rg.at[block, pl.ds(0, main), :, cols]
        remote(dst, dst, z_send.at[way, n], z_recv.at[way, n], (partner, j)).wait_recv()

    def z_wait_send(way, n):
        cols = pl.ds(pl.multiple_of((n % per) * CHUNK, CHUNK), CHUNK)
        src = right.at[pl.ds(0, main), :, cols]
        remote(src, src, z_send.at[way, n], z_recv.at[way, n], (partner, j)).wait_send()

    def e_copy(k):
        cols = pl.ds(k * CHUNK, CHUNK)
        return remote(right.at[pl.ds(main, rest), :, cols], rg.at[i, pl.ds(main, rest), :, cols],
                      e_send.at[k], e_recv.at[k], (partner, j))

    def m_start(r):
        cols = pl.ds(pl.multiple_of((r % per) * CHUNK, CHUNK), CHUNK)

        @pl.when(r < per)
        def _():
            remote(right.at[pl.ds(main, rest), :, cols], rg.at[i, pl.ds(main, rest), :, cols],
                   m_send.at[r], m_recv.at[r], (across, j)).start()

        @pl.when((r >= per) & (r < 2 * per))
        def _():
            block = rg.at[partner, pl.ds(main, rest), :, cols]
            remote(block, block, m_send.at[r], m_recv.at[r], (across, j)).start()

    def m_copy(r):
        cols = pl.ds(pl.multiple_of((r % per) * CHUNK, CHUNK), CHUNK)
        block = jnp.where(r < per, across, nz - 1 - partner)
        ref = rg.at[block, pl.ds(main, rest), :, cols]
        return remote(ref, ref, m_send.at[r], m_recv.at[r], (across, j))

    def le_copy(h):
        cols = pl.ds(h * half, half)
        return remote(left.at[:, :, cols], lg.at[1, j, :, :, cols],
                      le_send.at[h], le_recv.at[h], (partner, j))

    def te_copy():
        return remote(amps.at[:, pl.ds(main, rest), :], te, te_send, te_recv, (partner, j))

    def lg_copy(g, n):
        h0, h1 = pl.ds(0, half), pl.ds(half, half)
        src, to = (
            (lg.at[g, j], jx), (lg.at[g, j], jy), (lg.at[g, j], js),
            (lg.at[g, jx, :, :, h0], jy), (lg.at[g, jy, :, :, h1], jx),
            (lg.at[g, jx], js), (lg.at[g, jy], js), (lg.at[g, jd], js),
        )[n]
        return remote(src, src, lg_send.at[g, n], lg_recv.at[g, n], (i, to))

    def lg_first(g):
        for n in (0, 1, 2):
            lg_copy(g, n).start()

    def lg_second(g):
        for n in (0, 1):
            lg_copy(g, n).wait_recv()
        for n in (3, 4, 5, 6):
            lg_copy(g, n).start()

    def lg_third(g):
        for n in (3, 4):
            lg_copy(g, n).wait_recv()
        lg_copy(g, 7).start()

    def lg_last(g):
        for n in (2, 5, 6, 7):
            lg_copy(g, n).wait_recv()

    def load_left(g, block, k):
        vec = block * right_q + k * CHUNK
        src = lg.at[g, vec // left_q, :, :, pl.ds(pl.multiple_of(vec % left_q, CHUNK), CHUNK)]
        return pltpu.make_async_copy(src, lbuf, local.at[0])

    def load_right(block, k, start, size):
        src = rg.at[block, pl.ds(start, size), :, pl.ds(pl.multiple_of(k * CHUNK, CHUNK), CHUNK)]
        return pltpu.make_async_copy(src, rbuf.at[pl.ds(0, size)], local.at[1])

    def split_left():
        @pl.loop(0, count_a)
        def _(a):
            hi, lo = split(lbuf[a])
            rows = pl.ds(pl.multiple_of(a * count_c, count_c), count_c)
            ls[rows, 0:CHUNK] = hi
            ls[rows, CHUNK:2 * CHUNK] = lo
            ls[rows, 2 * CHUNK:3 * CHUNK] = hi

    def split_right(size):
        @pl.loop(0, size // 8)
        def _(g):
            hi, lo = split(rbuf[pl.ds(g * 8, 8)].reshape(8 * count_b, CHUNK))
            rows = pl.ds(pl.multiple_of(g * 8 * count_b, 8 * count_b), 8 * count_b)
            rs[rows, 0:CHUNK] = hi
            rs[rows, CHUNK:2 * CHUNK] = hi
            rs[rows, 2 * CHUNK:3 * CHUNK] = lo

    def multiply(target, rows):
        parts = 2 if rows > 1024 else 1
        size = rows // parts

        @pl.loop(0, count_a)
        def _(a):
            cols = pl.ds(pl.multiple_of(a * count_c, count_c), count_c)
            for part in range(parts):
                span = pl.ds(part * size, size)
                target[span, cols] += lax.dot_general(
                    rs[span, :], ls[cols, :], (((1,), (1,)), ((), ())),
                    preferred_element_type=jnp.float32)

    def main_task(block, k):
        a, b = load_left(0, block, k), load_right(block, k, 0, main)
        a.start()
        b.start()
        a.wait()
        split_left()
        b.wait()
        split_right(main)
        multiply(acc, rows_main)

    def rest_task(block, k):
        b = load_right(block, k, main, rest)
        b.start()
        a = load_left(0, block, k)
        a.start()
        b.wait()
        split_right(rest)
        a.wait()
        split_left()
        a = load_left(1, block, k)
        a.start()
        multiply(own_rest, rows_rest)
        a.wait()
        split_left()
        multiply(far_rest, rows_rest)

    for way in (0, 1):
        for n in range(AHEAD):
            z_start(way, n)
    keep_left = pltpu.make_async_copy(left, lg.at[0, j], local.at[0])
    keep_right = pltpu.make_async_copy(right, rg.at[i], local.at[1])
    keep_left.start()
    keep_right.start()

    @pl.when(is_end)
    def _():
        for h in (0, 1):
            le_copy(h).start()

    keep_left.wait()
    lg_first(0)

    @pl.loop(0, count_a)
    def _(a):
        cols = pl.ds(pl.multiple_of(a * count_c, count_c), count_c)
        acc[:, cols] = jnp.zeros((rows_main, count_c), jnp.float32)
        own_rest[:, cols] = jnp.zeros((rows_rest, count_c), jnp.float32)
        far_rest[:, cols] = jnp.zeros((rows_rest, count_c), jnp.float32)

    keep_right.wait()

    steps = (nz - 1) * per

    def last_task(t):
        return jnp.where(t < 5, 0, jnp.minimum(jnp.minimum(per + 6 * (t - 5), per + 2 * (t + 1)), per + 2 * steps))

    @pl.loop(0, 15)
    def _(t):
        for way in (0, 1):
            @pl.when(t < n_recv[way])
            def _(way=way):
                z_wait_recv(way, t)

        for way in (0, 1):
            @pl.when(t + AHEAD < n_send[way])
            def _(way=way):
                z_wait_send(way, t)

            z_start(way, t + AHEAD)

        @pl.when(is_end)
        def _():
            @pl.when(t == 3)
            def _():
                for k in range(2):
                    e_copy(k).start()

            @pl.when(t == 4)
            def _():
                for k in range(2, per):
                    e_copy(k).start()

            @pl.when(t == 6)
            def _():
                te_copy().start()

        @pl.when(t == 2)
        def _():
            lg_second(0)

        @pl.when((t == 3) & middle)
        def _():
            for h in (0, 1):
                le_copy(h).wait_recv()
            lg_first(1)

        @pl.when(t == 4)
        def _():
            lg_third(0)

        @pl.when(t == 5)
        def _():
            lg_last(0)

        @pl.when(middle)
        def _():
            @pl.when(t == 5)
            def _():
                lg_second(1)

            @pl.when(t == 6)
            def _():
                for r in range(AHEAD):
                    m_start(r)

            @pl.when(t == 7)
            def _():
                lg_third(1)

            @pl.when(t == 8)
            def _():
                lg_last(1)

            @pl.when(t == 9)
            def _():
                for k in range(per):
                    e_copy(k).wait_recv()

            @pl.when(t >= 7)
            def _():
                m_copy(t - 7).wait_send()
                m_start(t - 7 + AHEAD)
                m_copy(t - 7).wait_recv()

        def do_main(q, carry):
            u, way = (q - per) // 2, (q - per) % 2
            own = q < per
            block = jnp.where(own, i, jnp.where(way == 0, i - 1 - u // per, i + 1 + u // per))
            k = jnp.where(own, q, u % per)

            @pl.when(own | (u < jnp.where(way == 0, n_recv[0], n_recv[1])))
            def _():
                main_task(block, k)

            return carry

        lax.fori_loop(last_task(t - 1), last_task(t), do_main, 0)

        def do_rest(p, carry):
            source = p // per
            block = jnp.where(source == 0, i, jnp.where(source == 1, partner, jnp.where(
                source == 2, across, nz - 1 - partner)))
            rest_task(block, p % per)
            return carry

        def last_rest(t):
            return jnp.where(t < 8, 0, jnp.where(t < 11, per * (t - 7), t + 2))

        @pl.when(middle)
        def _():
            lax.fori_loop(last_rest(t - 1), last_rest(t), do_rest, 0)

    total[...] = jnp.zeros_like(total)

    def amplitude_pass(source, first, groups, totals):
        def fetch(g, slot):
            return pltpu.make_async_copy(
                source.at[:, pl.ds(pl.multiple_of(first + g * 8, 8), 8), :], tbuf.at[slot], tsem.at[slot])

        fetch(0, 0).start()

        @pl.loop(0, groups)
        def _(g):
            slot = g % 2

            @pl.when(g + 1 < groups)
            def _():
                fetch(g + 1, 1 - slot).start()

            fetch(g, slot).wait()
            flat = tbuf.at[slot].reshape(count_c * 8, tbuf.shape[-1])
            part = jnp.zeros(total.shape, jnp.float32)
            for d in range(8):
                t_hi, t_lo = split(flat[pl.ds(d, count_c, stride=8), :])
                rows = pl.ds(pl.multiple_of((g * 8 + d) * count_b, count_b), count_b)
                wide = totals[rows, :]
                tall = jnp.concatenate(
                    [wide[:, a * count_c:(a + 1) * count_c] for a in range(count_a)], axis=0)
                x_hi, x_lo = split(tall)
                part += jnp.dot(
                    jnp.concatenate([x_hi, x_hi, x_lo], axis=1),
                    jnp.concatenate([t_hi, t_lo, t_hi], axis=0),
                    preferred_element_type=jnp.float32)
            total[...] += part

    amplitude_pass(amps, 0, main // 8, acc)

    @pl.when(middle)
    def _():
        amplitude_pass(amps, main, rest // 8, own_rest)
        te_copy().wait_recv()
        amplitude_pass(te, 0, rest // 8, far_rest)

    total[...] = total[...].T

    size = out.shape[0]

    def d_copy(step, src_rows, slot, who):
        return remote(total.at[pl.ds(pl.multiple_of(src_rows * size, size), size)], red_d.at[slot],
                      d_send.at[step], d_recv.at[step], (i, who))

    for step in range(1, nd):
        to = (j + step) % nd
        d_copy(step, to, step, to).start()
    red_d[0] = total[pl.ds(pl.multiple_of(j * size, size), size), :]
    for step in range(1, nd):
        d_copy(step, j, step, js).wait_recv()
    here = red_d[0]
    for step in range(1, nd):
        here = here + red_d[step]
    red_c[0] = here

    def c_copy(step):
        return remote(red_c.at[0], red_c.at[step], c_send.at[step], c_recv.at[step], ((i + step) % nz, j))

    for step in range(1, nz):
        c_copy(step).start()
    for step in range(1, nz):
        c_copy(step).wait_recv()
    for step in range(1, nz):
        here = here + red_c[step]
    out[...] = here

    for step in range(1, nz):
        c_copy(step).wait_send()
    for step in range(1, nd):
        d_copy(step, j, step, js).wait_send()
    for n in range(8):
        lg_copy(0, n).wait_send()

    @pl.when(middle)
    def _():
        for n in range(8):
            lg_copy(1, n).wait_send()

    @pl.when(is_end)
    def _():
        for h in (0, 1):
            le_copy(h).wait_send()
        for k in range(per):
            e_copy(k).wait_send()
        te_copy().wait_send()

    for way in (0, 1):
        @pl.when(n_send[way] > 0)
        def _(way=way):
            for n in range(AHEAD):
                z_wait_send(way, n_send[way] - AHEAD + n)


def shards(nz, nd, main, vectors_left, vectors_right, amplitudes):
    count_a, count_c, left_q = vectors_left.shape
    count_b, count_d, right_q = vectors_right.shape
    pairs = amplitudes.shape[2]
    rest = count_d - main
    per = right_q // CHUNK
    f32, bf16 = jnp.float32, jnp.bfloat16
    columns = count_a * count_c
    dma = pltpu.SemaphoreType.DMA
    hbm = pl.BlockSpec(memory_space=pl.ANY)
    results = pl.pallas_call(
        functools.partial(kernel, nz, nd, main),
        out_shape=[
            jax.ShapeDtypeStruct((pairs // nd, count_a * count_b), f32),
            jax.ShapeDtypeStruct((2, nd, count_a, count_c, left_q), f32),
            jax.ShapeDtypeStruct((nz, count_d, count_b, right_q), f32),
            jax.ShapeDtypeStruct((count_c, rest, pairs), f32),
        ],
        in_specs=[hbm] * 3,
        out_specs=[pl.BlockSpec(memory_space=pltpu.VMEM), hbm, hbm, hbm],
        scratch_shapes=[
            pltpu.VMEM((main * count_b, columns), f32),
            pltpu.VMEM((rest * count_b, columns), f32),
            pltpu.VMEM((rest * count_b, columns), f32),
            pltpu.VMEM((count_a, count_c, CHUNK), f32),
            pltpu.VMEM((main, count_b, CHUNK), f32),
            pltpu.VMEM((columns, 3 * CHUNK), bf16),
            pltpu.VMEM((main * count_b, 3 * CHUNK), bf16),
            pltpu.VMEM((2, count_c, 8, pairs), f32),
            pltpu.VMEM((count_a * count_b, pairs), f32),
            pltpu.VMEM((nd, pairs // nd, count_a * count_b), f32),
            pltpu.VMEM((nz, pairs // nd, count_a * count_b), f32),
            dma((2, (nz - 1) * per)), dma((2, (nz - 1) * per)),
            dma((2 * per,)), dma((2 * per,)),
            dma((per,)), dma((per,)),
            dma((2,)), dma((2,)),
            dma, dma,
            dma((2, 8)), dma((2, 8)),
            dma((nd,)), dma((nd,)),
            dma((nz,)), dma((nz,)),
            dma((2,)), dma((2,)),
        ],
        compiler_params=pltpu.CompilerParams(
            collective_id=0, has_side_effects=True, vmem_limit_bytes=52 * 2**20),
        name="ladder",
    )(vectors_left, jnp.transpose(vectors_right, (1, 0, 2)), amplitudes)
    whole = results[0].reshape(pairs // nd, count_a, count_b)
    width = count_b // nz
    return lax.dynamic_slice_in_dim(whole, lax.axis_index("vc") * width, width, axis=2)


def solution(mesh):
    nz, nd = mesh.shape["vc"], mesh.shape["vd"]
    fits = nz == 4 and nd == 8
    body = functools.partial(shards, nz, nd, 88) if fits else plain
    return jax.shard_map(
        body,
        mesh=mesh,
        in_specs=(P(None, "vc", "vd"), P(None, "vd", "vc"), P("vc", "vd", None)),
        out_specs=P("vd", None, "vc"),
        check_vma=False,
    )
```

time: 1050 us -> 895 us (0.85)
  Pallas kernels: 0 us -> 881 us
  waiting for transfers between devices: 780 us -> 0 us
  matrix products: 256 us -> 0 us
  between operations: 13.1 us -> 0.01 us
    pallas_call x0 -> x1, Pallas kernels: none -> 881 us  [shards(): pl.pallas_call(functools.partial(kernel, nz, nd, main), out_shape=[jax.Sh...]
    all_gather x2 -> x0, waiting for transfers between devices: 726 us -> none  [the longest x1 565 us: shards(): piece = lax.all_gather(vectors_right, 'vc', axis=2, tiled=True)]
    dot_general x2 -> x0, matrix products: 256 us -> none  [the longest x1 222 us: contract(): lax.dot_general(left_rows, right_rows, (((1,), (1,)), ((), ())), precisio...]
    unnamed x5 -> x0, waiting for transfers between devices: 34.8 us -> none
    reduce_scatter x1 -> x0, waiting for transfers between devices: 19.8 us -> none  [shards(): ladder = lax.psum_scatter(reduced, 'vc', scatter_dimension=2, tiled=True)]
  transfers between devices with their start and end apart: 4 -> 0, of which waited for: 4 -> 0; matrix products, arithmetic and copies ran while one was open for 0% -> 0% of each run, Pallas kernels for 0% -> 0%
where the time goes in v1:
time: 895 us; the launch traced here: 894 us
  Pallas kernels  881 us (98%)
  local copies, waits for them, and re-layouts  12.3 us (1%)
    pallas_call x1, Pallas kernels, shards(): pl.pallas_call(functools.partial(kernel, nz, nd, main), out_shape=[jax.Sh...  881 us

profile of v1, /device:TPU:0, one launch (start us, length us, event | category | flops | bytes accessed | tf_op | source)
XLA Modules:
  0.0 893.7 jit_solution(4255167438525509675)
XLA Ops:
  0.0 11.5 %copy.8 = f32[16,128,1024]{2,0,1:T(8,128)} copy(f32[16,128,1024]{2,1,0:T(8,128)} %param.4) | data formatting | bytes 16777216 | tf_op args[1]
  11.5 881.5 %ladder.1 = (f32[16,128]{1,0:T(8,128)S(1)}, f32[2,8,8,256,512]{4,3,2,1,0:T(8,128)}, f32[4,128,16,1024]{3,2,1,0:T(8,128)}, f32[256,40,128]{2,1,0:T(8,128)}) custom-call(f32[8,256,512]{2,1,0:T(8,128)} %left.1, f32[128,16,1024]{2,1,0:T(8,128)} %bitcast.4, f32[256,128,128]{2,1,0:T(8,128)} %amps.1), custom_call_target="tpu_custom_call" | custom-call | tf_op jit(solution)/shard_map/ladder/pallas_call | solution.py:478
  893.0 0.1 copy.6
  893.1 0.6 constant_dynamic-slice_fusion

commit v2 on v1

--- a/solution.py
+++ b/solution.py
@@ -9,7 +9,8 @@
 
 MESH = pl.DeviceIdType.MESH
 CHUNK = 256
-AHEAD = 2
+AHEAD = 3
+AHEAD_REST = 2
 
 
 def contract(left_rows, right_rows):
@@ -45,12 +46,12 @@
 def kernel(nz, nd, main, left, right, amps, out, lg, rg, te, acc, own_rest, far_rest,
            lbuf, rbuf, ls, rs, tbuf, total, red_d, red_c,
            z_send, z_recv, m_send, m_recv, e_send, e_recv, le_send, le_recv, te_send, te_recv,
-           lg_send, lg_recv, d_send, d_recv, c_send, c_recv, local, tsem):
+           lg_send, lg_recv, d_send, d_recv, c_send, c_recv, local, tsem, keep):
     count_a, count_c, left_q = left.shape
     count_d, count_b, right_q = right.shape
+    per = right_q // CHUNK
     rest = count_d - main
-    per = right_q // CHUNK
-    half = left_q // 2
+    halves = left_q // CHUNK
     rows_main, rows_rest = main * count_b, rest * count_b
     i = lax.axis_index("vc")
     j = lax.axis_index("vd")
@@ -77,11 +78,14 @@
     n_send = (jnp.where(i < nz - 1, per * (i + 1), 0), jnp.where(i > 0, per * (nz - i), 0))
     n_recv = (per * i, per * (nz - 1 - i))
 
+    def mine(k, start, size):
+        cols = pl.ds(pl.multiple_of(k * CHUNK, CHUNK), CHUNK)
+        return right.at[pl.ds(start, size), :, cols]
+
     def z_copy(way, n, src_own):
         block = jnp.where(way == 0, i - n // per, i + n // per) if src_own is None else i
-        cols = pl.ds(pl.multiple_of((n % per) * CHUNK, CHUNK), CHUNK)
-        dst = rg.at[block, pl.ds(0, main), :, cols]
-        src = right.at[pl.ds(0, main), :, cols] if src_own else dst
+        dst = rg.at[block, n % per, pl.ds(0, main)]
+        src = mine(n % per, 0, main) if src_own else dst
         who = (i + 1, j) if way == 0 else (i - 1, j)
         return remote(src, dst, z_send.at[way, n], z_recv.at[way, n], who)
 
@@ -96,52 +100,45 @@
 
     def z_wait_recv(way, n):
         block = i - 1 - n // per if way == 0 else i + 1 + n // per
-        cols = pl.ds(pl.multiple_of((n % per) * CHUNK, CHUNK), CHUNK)
-        dst = rg.at[block, pl.ds(0, main), :, cols]
+        dst = rg.at[block, n % per, pl.ds(0, main)]
         remote(dst, dst, z_send.at[way, n], z_recv.at[way, n], (partner, j)).wait_recv()
 
     def z_wait_send(way, n):
-        cols = pl.ds(pl.multiple_of((n % per) * CHUNK, CHUNK), CHUNK)
-        src = right.at[pl.ds(0, main), :, cols]
+        src = mine(n % per, 0, main)
         remote(src, src, z_send.at[way, n], z_recv.at[way, n], (partner, j)).wait_send()
 
     def e_copy(k):
-        cols = pl.ds(k * CHUNK, CHUNK)
-        return remote(right.at[pl.ds(main, rest), :, cols], rg.at[i, pl.ds(main, rest), :, cols],
+        return remote(mine(k, main, rest), rg.at[i, k, pl.ds(main, rest)],
                       e_send.at[k], e_recv.at[k], (partner, j))
 
     def m_start(r):
-        cols = pl.ds(pl.multiple_of((r % per) * CHUNK, CHUNK), CHUNK)
-
         @pl.when(r < per)
         def _():
-            remote(right.at[pl.ds(main, rest), :, cols], rg.at[i, pl.ds(main, rest), :, cols],
+            remote(mine(r % per, main, rest), rg.at[i, r % per, pl.ds(main, rest)],
                    m_send.at[r], m_recv.at[r], (across, j)).start()
 
         @pl.when((r >= per) & (r < 2 * per))
         def _():
-            block = rg.at[partner, pl.ds(main, rest), :, cols]
+            block = rg.at[partner, r % per, pl.ds(main, rest)]
             remote(block, block, m_send.at[r], m_recv.at[r], (across, j)).start()
 
     def m_copy(r):
-        cols = pl.ds(pl.multiple_of((r % per) * CHUNK, CHUNK), CHUNK)
         block = jnp.where(r < per, across, nz - 1 - partner)
-        ref = rg.at[block, pl.ds(main, rest), :, cols]
+        ref = rg.at[block, r % per, pl.ds(main, rest)]
         return remote(ref, ref, m_send.at[r], m_recv.at[r], (across, j))
 
     def le_copy(h):
-        cols = pl.ds(h * half, half)
-        return remote(left.at[:, :, cols], lg.at[1, j, :, :, cols],
+        return remote(lg.at[0, j, h], lg.at[1, j, h],
                       le_send.at[h], le_recv.at[h], (partner, j))
 
     def te_copy():
         return remote(amps.at[:, pl.ds(main, rest), :], te, te_send, te_recv, (partner, j))
 
     def lg_copy(g, n):
-        h0, h1 = pl.ds(0, half), pl.ds(half, half)
+        h0, h1 = pl.ds(0, halves // 2), pl.ds(halves // 2, halves // 2)
         src, to = (
             (lg.at[g, j], jx), (lg.at[g, j], jy), (lg.at[g, j], js),
-            (lg.at[g, jx, :, :, h0], jy), (lg.at[g, jy, :, :, h1], jx),
+            (lg.at[g, jx, h0], jy), (lg.at[g, jy, h1], jx),
             (lg.at[g, jx], js), (lg.at[g, jy], js), (lg.at[g, jd], js),
         )[n]
         return remote(src, src, lg_send.at[g, n], lg_recv.at[g, n], (i, to))
@@ -166,22 +163,22 @@
             lg_copy(g, n).wait_recv()
 
     def load_left(g, block, k):
-        vec = block * right_q + k * CHUNK
-        src = lg.at[g, vec // left_q, :, :, pl.ds(pl.multiple_of(vec % left_q, CHUNK), CHUNK)]
+        chunk = block * per + k
+        src = lg.at[g, chunk // halves, chunk % halves]
         return pltpu.make_async_copy(src, lbuf, local.at[0])
 
     def load_right(block, k, start, size):
-        src = rg.at[block, pl.ds(start, size), :, pl.ds(pl.multiple_of(k * CHUNK, CHUNK), CHUNK)]
+        src = rg.at[block, k, pl.ds(start, size)]
         return pltpu.make_async_copy(src, rbuf.at[pl.ds(0, size)], local.at[1])
 
     def split_left():
         @pl.loop(0, count_a)
         def _(a):
             hi, lo = split(lbuf[a])
-            rows = pl.ds(pl.multiple_of(a * count_c, count_c), count_c)
-            ls[rows, 0:CHUNK] = hi
-            ls[rows, CHUNK:2 * CHUNK] = lo
-            ls[rows, 2 * CHUNK:3 * CHUNK] = hi
+            cols = pl.ds(pl.multiple_of(a * count_c, count_c), count_c)
+            ls[0:CHUNK, cols] = hi
+            ls[CHUNK:2 * CHUNK, cols] = lo
+            ls[2 * CHUNK:3 * CHUNK, cols] = hi
 
     def split_right(size):
         @pl.loop(0, size // 8)
@@ -201,9 +198,8 @@
             cols = pl.ds(pl.multiple_of(a * count_c, count_c), count_c)
             for part in range(parts):
                 span = pl.ds(part * size, size)
-                target[span, cols] += lax.dot_general(
-                    rs[span, :], ls[cols, :], (((1,), (1,)), ((), ())),
-                    preferred_element_type=jnp.float32)
+                target[span, cols] += jnp.dot(
+                    rs[span, :], ls[:, cols], preferred_element_type=jnp.float32)
 
     def main_task(block, k):
         a, b = load_left(0, block, k), load_right(block, k, 0, main)
@@ -234,17 +230,27 @@
     for way in (0, 1):
         for n in range(AHEAD):
             z_start(way, n)
-    keep_left = pltpu.make_async_copy(left, lg.at[0, j], local.at[0])
-    keep_right = pltpu.make_async_copy(right, rg.at[i], local.at[1])
-    keep_left.start()
-    keep_right.start()
-
-    @pl.when(is_end)
-    def _():
-        for h in (0, 1):
+    keep_right = [pltpu.make_async_copy(mine(k, 0, count_d), rg.at[i, k], keep.at[k]) for k in range(per)]
+    for copy in keep_right:
+        copy.start()
+
+    for h in range(halves):
+        take = pltpu.make_async_copy(left.at[:, :, pl.ds(h * CHUNK, CHUNK)], lbuf, local.at[0])
+        take.start()
+        take.wait()
+
+        @pl.loop(0, count_a)
+        def _(a):
+            lbuf[a] = lbuf[a].T
+
+        give = pltpu.make_async_copy(lbuf, lg.at[0, j, h], local.at[0])
+        give.start()
+        give.wait()
+
+        @pl.when(is_end)
+        def _(h=h):
             le_copy(h).start()
 
-    keep_left.wait()
     lg_first(0)
 
     @pl.loop(0, count_a)
@@ -254,7 +260,8 @@
         own_rest[:, cols] = jnp.zeros((rows_rest, count_c), jnp.float32)
         far_rest[:, cols] = jnp.zeros((rows_rest, count_c), jnp.float32)
 
-    keep_right.wait()
+    for copy in keep_right:
+        copy.wait()
 
     steps = (nz - 1) * per
 
@@ -297,7 +304,7 @@
 
         @pl.when((t == 3) & middle)
         def _():
-            for h in (0, 1):
+            for h in range(halves):
                 le_copy(h).wait_recv()
             lg_first(1)
 
@@ -317,7 +324,7 @@
 
             @pl.when(t == 6)
             def _():
-                for r in range(AHEAD):
+                for r in range(AHEAD_REST):
                     m_start(r)
 
             @pl.when(t == 7)
@@ -336,7 +343,7 @@
             @pl.when(t >= 7)
             def _():
                 m_copy(t - 7).wait_send()
-                m_start(t - 7 + AHEAD)
+                m_start(t - 7 + AHEAD_REST)
                 m_copy(t - 7).wait_recv()
 
         def do_main(q, carry):
@@ -452,7 +459,7 @@
 
     @pl.when(is_end)
     def _():
-        for h in (0, 1):
+        for h in range(halves):
             le_copy(h).wait_send()
         for k in range(per):
             e_copy(k).wait_send()
@@ -479,8 +486,8 @@
         functools.partial(kernel, nz, nd, main),
         out_shape=[
             jax.ShapeDtypeStruct((pairs // nd, count_a * count_b), f32),
-            jax.ShapeDtypeStruct((2, nd, count_a, count_c, left_q), f32),
-            jax.ShapeDtypeStruct((nz, count_d, count_b, right_q), f32),
+            jax.ShapeDtypeStruct((2, nd, left_q // CHUNK, count_a, CHUNK, count_c), f32),
+            jax.ShapeDtypeStruct((nz, per, count_d, count_b, CHUNK), f32),
             jax.ShapeDtypeStruct((count_c, rest, pairs), f32),
         ],
         in_specs=[hbm] * 3,
@@ -489,9 +496,9 @@
             pltpu.VMEM((main * count_b, columns), f32),
             pltpu.VMEM((rest * count_b, columns), f32),
             pltpu.VMEM((rest * count_b, columns), f32),
-            pltpu.VMEM((count_a, count_c, CHUNK), f32),
+            pltpu.VMEM((count_a, CHUNK, count_c), f32),
             pltpu.VMEM((main, count_b, CHUNK), f32),
-            pltpu.VMEM((columns, 3 * CHUNK), bf16),
+            pltpu.VMEM((3 * CHUNK, columns), bf16),
             pltpu.VMEM((main * count_b, 3 * CHUNK), bf16),
             pltpu.VMEM((2, count_c, 8, pairs), f32),
             pltpu.VMEM((count_a * count_b, pairs), f32),
@@ -505,7 +512,7 @@
             dma((2, 8)), dma((2, 8)),
             dma((nd,)), dma((nd,)),
             dma((nz,)), dma((nz,)),
-            dma((2,)), dma((2,)),
+            dma((2,)), dma((2,)), dma((per,)),
         ],
         compiler_params=pltpu.CompilerParams(
             collective_id=0, has_side_effects=True, vmem_limit_bytes=52 * 2**20),

time: 895 us -> 733 us (0.82)
  Pallas kernels: 881 us -> 719 us
    pallas_call x1, Pallas kernels: 881 us -> 719 us  [shards(): pl.pallas_call(functools.partial(kernel, nz, nd, main), out_shape=[jax.Sh...]
where the time goes in v2:
time: 733 us; the launch traced here: 732 us
  Pallas kernels  719 us (98%)
  local copies, waits for them, and re-layouts  12.3 us (2%)
    pallas_call x1, Pallas kernels, shards(): pl.pallas_call(functools.partial(kernel, nz, nd, main), out_shape=[jax.Sh...  719 us

profile of v2, /device:TPU:0, one launch (start us, length us, event | category | flops | bytes accessed | tf_op | source)
XLA Modules:
  0.0 731.6 jit_solution(1589808177437172066)
XLA Ops:
  0.0 11.5 %copy.8 = f32[16,128,1024]{2,0,1:T(8,128)} copy(f32[16,128,1024]{2,1,0:T(8,128)} %param.4) | data formatting | bytes 16777216 | tf_op args[1]
  11.5 719.3 %ladder.1 = (f32[16,128]{1,0:T(8,128)S(1)}, f32[2,8,2,8,256,256]{5,4,3,2,1,0:T(8,128)}, f32[4,4,128,16,256]{4,3,2,1,0:T(8,128)}, f32[256,40,128]{2,1,0:T(8,128)}) custom-call(f32[8,256,512]{2,1,0:T(8,128)} %left.1, f32[128,16,1024]{2,1,0:T(8,128)} %bitcast.4, f32[256,128,128]{2,1,0:T(8,128)} %amps.1), custom_call_target="tpu_custom_call" | custom-call | tf_op jit(solution)/shard_map/ladder/pallas_call | solution.py:485
  730.9 0.1 copy.6
  731.0 0.6 constant_dynamic-slice_fusion

commit v3 on v2

v3 whole, which is shorter than its diff:
```python
import functools

import jax
import jax.numpy as jnp
from jax import lax
from jax.experimental import pallas as pl
from jax.experimental.pallas import tpu as pltpu
from jax.sharding import PartitionSpec as P

MESH = pl.DeviceIdType.MESH
CHUNK = 256
AHEAD = 2


def contract(left_rows, right_rows):
    return lax.dot_general(
        left_rows,
        right_rows,
        (((1,), (1,)), ((), ())),
        precision=lax.Precision.HIGHEST,
        preferred_element_type=jnp.float32,
    )


def plain(vectors_left, vectors_right, amplitudes):
    count_a, count_c, left_q = vectors_left.shape
    count_b, count_d, right_q = vectors_right.shape
    left_whole = lax.all_gather(vectors_left, "vd", axis=2, tiled=True)
    left_flat = left_whole.reshape(count_a * count_c, left_whole.shape[2])
    piece = lax.all_gather(vectors_right, "vc", axis=2, tiled=True)
    width = piece.shape[2]
    tile = contract(left_flat, piece.reshape(count_b * count_d, width))
    tile = tile.reshape(count_a, count_c, count_b, count_d)
    partial_sum = jnp.einsum("acbd,cdi->iab", tile, amplitudes, precision=lax.Precision.HIGHEST)
    reduced = lax.psum_scatter(partial_sum, "vd", scatter_dimension=0, tiled=True)
    return lax.psum_scatter(reduced, "vc", scatter_dimension=2, tiled=True)


def split(x):
    hi = x.astype(jnp.bfloat16)
    lo = (x - hi.astype(jnp.float32)).astype(jnp.bfloat16)
    return hi, lo


def kernel(nz, nd, main, left, right, amps, out, lg, rg, te, acc, far,
           lbuf, rbuf, ls, rs, tbuf, total, red_d, red_c,
           in_send, in_recv, m_send, m_recv, e_send, e_recv, le_send, le_recv, te_send, te_recv,
           lg_send, lg_recv, d_send, d_recv, c_send, c_recv, local, tsem, keep):
    count_a, count_c, left_q = left.shape
    count_d, count_b, right_q = right.shape
    per = right_q // CHUNK
    rest = count_d - main
    halves = left_q // CHUNK
    rows_main, rows_rest = main * count_b, rest * count_b
    i = lax.axis_index("vc")
    j = lax.axis_index("vd")
    core, x, y = j % 2, (j // 2) % 2, j // 4
    jx, jy, js = j + 2 - 4 * x, j + 4 - 8 * y, j + 1 - 2 * core
    jd = jx + 4 - 8 * y
    is_end = (i == 0) | (i == nz - 1)
    middle = jnp.logical_not(is_end)
    partner = jnp.where(i < nz // 2, 1 - i, 2 * nz - 3 - i)
    across = nz - 1 - i

    barrier = pltpu.get_barrier_semaphore()
    for step in range(1, nd):
        pl.semaphore_signal(barrier, inc=1, device_id=(i, (j + step) % nd), device_id_type=MESH)
    for step in range(1, nz):
        pl.semaphore_signal(barrier, inc=1, device_id=((i + step) % nz, j), device_id_type=MESH)
    pl.semaphore_wait(barrier, nd - 1 + nz - 1)

    def remote(src, dst, send, recv, who):
        return pltpu.make_async_remote_copy(
            src_ref=src, dst_ref=dst, send_sem=send, recv_sem=recv, device_id=who, device_id_type=MESH)

    def mine(k, start, size):
        cols = pl.ds(pl.multiple_of(k * CHUNK, CHUNK), CHUNK)
        return right.at[pl.ds(start, size), :, cols]

    def in_copy(n, own):
        dst = rg.at[jnp.where(n < per, i, jnp.where(n < 2 * per, across, nz - 1 - partner)), n % per, pl.ds(0, main)]
        return remote(mine(n, 0, main) if own else dst, dst, in_send.at[n], in_recv.at[n], (partner, j))

    def e_copy(k):
        return remote(mine(k, 0, count_d), rg.at[i, k], e_send.at[k], e_recv.at[k], (partner, j))

    def m_start(n):
        @pl.when(n < per)
        def _():
            remote(mine(n, 0, count_d), rg.at[i, n], m_send.at[n], m_recv.at[n], (across, j)).start()

        @pl.when(n >= per)
        def _():
            block = rg.at[partner, n % per]
            remote(block, block, m_send.at[n], m_recv.at[n], (across, j)).start()

    def m_copy(n):
        ref = rg.at[jnp.where(n < per, across, nz - 1 - partner), n % per]
        return remote(ref, ref, m_send.at[n], m_recv.at[n], (across, j))

    def le_copy(h):
        return remote(lg.at[0, j, h], lg.at[1, j, h],
                      le_send.at[h], le_recv.at[h], (partner, j))

    def te_copy():
        return remote(amps.at[:, pl.ds(main, rest), :], te, te_send, te_recv, (partner, j))

    def lg_copy(g, n):
        h0, h1 = pl.ds(0, halves // 2), pl.ds(halves // 2, halves // 2)
        src, to = (
            (lg.at[g, j], jx), (lg.at[g, j], jy), (lg.at[g, j], js),
            (lg.at[g, jx, h0], jy), (lg.at[g, jy, h1], jx),
            (lg.at[g, jx], js), (lg.at[g, jy], js), (lg.at[g, jd], js),
        )[n]
        return remote(src, src, lg_send.at[g, n], lg_recv.at[g, n], (i, to))

    def lg_first(g):
        for n in (0, 1, 2):
            lg_copy(g, n).start()

    def lg_second(g):
        for n in (0, 1):
            lg_copy(g, n).wait_recv()
        for n in (3, 4, 5, 6):
            lg_copy(g, n).start()

    def lg_third(g):
        for n in (3, 4):
            lg_copy(g, n).wait_recv()
        lg_copy(g, 7).start()

    def lg_last(g):
        for n in (2, 5, 6, 7):
            lg_copy(g, n).wait_recv()

    def load_left(g, block, k):
        chunk = block * per + k
        src = lg.at[g, chunk // halves, chunk % halves]
        return pltpu.make_async_copy(src, lbuf, local.at[0])

    def load_right(block, k, start, size):
        src = rg.at[block, k, pl.ds(start, size)]
        return pltpu.make_async_copy(src, rbuf.at[pl.ds(start, size)], local.at[1 if start == 0 else 2])

    def split_left():
        @pl.loop(0, count_a)
        def _(a):
            hi, lo = split(lbuf[a])
            cols = pl.ds(pl.multiple_of(a * count_c, count_c), count_c)
            ls[0:CHUNK, cols] = hi
            ls[CHUNK:2 * CHUNK, cols] = lo
            ls[2 * CHUNK:3 * CHUNK, cols] = hi

    def split_right(start, size):
        @pl.loop(start // 8, (start + size) // 8)
        def _(g):
            hi, lo = split(rbuf[pl.ds(g * 8, 8)].reshape(8 * count_b, CHUNK))
            rows = pl.ds(pl.multiple_of(g * 8 * count_b, 8 * count_b), 8 * count_b)
            rs[rows, 0:CHUNK] = hi
            rs[rows, CHUNK:2 * CHUNK] = hi
            rs[rows, 2 * CHUNK:3 * CHUNK] = lo

    def multiply(target, spans):
        @pl.loop(0, count_a)
        def _(a):
            cols = pl.ds(pl.multiple_of(a * count_c, count_c), count_c)
            for start, first, size in spans:
                target[pl.ds(start, size), cols] += jnp.dot(
                    rs[pl.ds(first, size), :], ls[:, cols], preferred_element_type=jnp.float32)

    half = rows_main // 2
    main_spans = ((0, 0, half), (half, half, half))
    rest_spans = main_spans + ((rows_main, rows_main, rows_rest),)
    far_spans = ((0, rows_main, rows_rest),)

    def run(first, last, where, g, parts, target, spans):
        def loads(q):
            block, k = where(q)
            return [load_left(g, block, k)] + [load_right(block, k, *part) for part in parts]

        @pl.when(first < last)
        def _():
            for copy in loads(first):
                copy.start()

        def task(q, carry):
            for copy in loads(q):
                copy.wait()
            split_left()
            for part in parts:
                split_right(*part)

            @pl.when(q + 1 < last)
            def _():
                for copy in loads(q + 1):
                    copy.start()

            multiply(target, spans)
            return carry

        lax.fori_loop(first, last, task, 0)

    def from_middle(n):
        return jnp.where(n < per, across, nz - 1 - partner), n % per

    def from_partner(n):
        return jnp.where(i == 0, 1 + n // per, nz - 2 - n // per), n % per

    def end_task(q):
        block, k = from_partner(q - per)
        return jnp.where(q < per, i, block), jnp.where(q < per, q, k)

    def middle_task(q):
        r = q - per - 3
        from_end = (r >= 0) & (r < 7) & (r % 2 == 0)
        n = jnp.where(r < 0, q - per, jnp.where(r < 7, 3 + r // 2, q - 2 * per))
        block, k = from_middle(n)
        block, k = jnp.where(from_end, partner, block), jnp.where(from_end, r // 2, k)
        return jnp.where(q < per, i, block), jnp.where(q < per, q, k)

    def far_task(q):
        block, k = from_middle(q - 2 * per)
        return jnp.where(q < per, i, jnp.where(q < 2 * per, partner, block)), jnp.where(q < 2 * per, q % per, k)

    @pl.when(is_end)
    def _():
        e_copy(0).start()

    @pl.when(middle)
    def _():
        for n in range(AHEAD):
            m_start(n)
        for n in range(per):
            in_copy(n, True).start()

    keep_right = [pltpu.make_async_copy(mine(k, 0, count_d), rg.at[i, k], keep.at[k]) for k in range(per)]
    for copy in keep_right:
        copy.start()

    for h in range(halves):
        take = pltpu.make_async_copy(left.at[:, :, pl.ds(h * CHUNK, CHUNK)], lbuf, local.at[0])
        take.start()
        take.wait()

        @pl.loop(0, count_a)
        def _(a):
            lbuf[a] = lbuf[a].T

        give = pltpu.make_async_copy(lbuf, lg.at[0, j, h], local.at[0])
        give.start()
        give.wait()

        @pl.when(is_end)
        def _(h=h):
            le_copy(h).start()

    lg_first(0)

    @pl.loop(0, count_a)
    def _(a):
        cols = pl.ds(pl.multiple_of(a * count_c, count_c), count_c)
        acc[:, cols] = jnp.zeros((rows_main + rows_rest, count_c), jnp.float32)
        far[:, cols] = jnp.zeros((rows_rest, count_c), jnp.float32)

    for copy in keep_right:
        copy.wait()

    @pl.when(is_end)
    def _():
        @pl.loop(0, (nz - 1) * per)
        def _(t):
            block, k = from_partner(t)
            ref = rg.at[block, k, pl.ds(0, main)]
            remote(ref, ref, in_send.at[t], in_recv.at[t], (partner, j)).wait_recv()

            @pl.when(t == 2)
            def _():
                e_copy(1).start()
                lg_second(0)

            @pl.when(t == 3)
            def _():
                lg_third(0)

            @pl.when(t == 4)
            def _():
                e_copy(2).start()
                lg_last(0)

            @pl.when(t == 5)
            def _():
                e_copy(3).start()

            @pl.when(t == 7)
            def _():
                te_copy().start()

            def last(t):
                return jnp.where(t < 4, 0, jnp.minimum(t + 5, 4 * t - 10))

            run(last(t - 1), last(t), end_task, 0, ((0, main),), acc, main_spans)

    @pl.when(middle)
    def _():
        @pl.loop(0, 2 * per)
        def _(t):
            m_copy(t).wait_recv()
            in_copy(t + per, False).start()

            @pl.when(t + AHEAD < 2 * per)
            def _():
                m_copy(t).wait_send()

                @pl.when(t + AHEAD >= per)
                def _():
                    e_copy(t + AHEAD - per).wait_recv()

                m_start(t + AHEAD)

            @pl.when(t == 1)
            def _():
                lg_second(0)

            @pl.when(t == 2)
            def _():
                lg_third(0)
                for h in range(halves):
                    le_copy(h).wait_recv()
                lg_first(1)
                lg_last(0)

            @pl.when(t == 4)
            def _():
                lg_second(1)

            @pl.when(t == 5)
            def _():
                lg_third(1)
                lg_last(1)

            def last(t):
                late = jnp.where(t < 6, 4 + 2 * t, 9 + t)
                return jnp.where(t < 2, 0, jnp.where(t == 2, 7, late))

            def last_far(t):
                return jnp.where(t < 5, 0, jnp.where(t < 7, 5 * t - 19, 16))

            run(last(t - 1), last(t), middle_task, 0, ((0, main), (main, rest)), acc, rest_spans)
            run(last_far(t - 1), last_far(t), far_task, 1, ((main, rest),), far, far_spans)

    total[...] = jnp.zeros_like(total)

    def amplitude_pass(source, first, groups, totals):
        def fetch(g, slot):
            return pltpu.make_async_copy(
                source.at[:, pl.ds(pl.multiple_of(first + g * 8, 8), 8), :], tbuf.at[slot], tsem.at[slot])

        fetch(0, 0).start()

        @pl.loop(0, groups)
        def _(g):
            slot = g % 2

            @pl.when(g + 1 < groups)
            def _():
                fetch(g + 1, 1 - slot).start()

            fetch(g, slot).wait()
            flat = tbuf.at[slot].reshape(count_c * 8, tbuf.shape[-1])
            part = jnp.zeros(total.shape, jnp.float32)
            for d in range(8):
                t_hi, t_lo = split(flat[pl.ds(d, count_c, stride=8), :])
                rows = pl.ds(pl.multiple_of((g * 8 + d) * count_b, count_b), count_b)
                wide = totals[rows, :]
                tall = jnp.concatenate(
                    [wide[:, a * count_c:(a + 1) * count_c] for a in range(count_a)], axis=0)
                x_hi, x_lo = split(tall)
                part += jnp.dot(
                    jnp.concatenate([x_hi, x_hi, x_lo], axis=1),
                    jnp.concatenate([t_hi, t_lo, t_hi], axis=0),
                    preferred_element_type=jnp.float32)
            total[...] += part

    amplitude_pass(amps, 0, jnp.where(middle, count_d // 8, main // 8), acc)

    @pl.when(middle)
    def _():
        te_copy().wait_recv()
        amplitude_pass(te, 0, rest // 8, far)

    total[...] = total[...].T

    size = out.shape[0]

    def d_copy(step, src_rows, slot, who):
        return remote(total.at[pl.ds(pl.multiple_of(src_rows * size, size), size)], red_d.at[slot],
                      d_send.at[step], d_recv.at[step], (i, who))

    for step in range(1, nd):
        to = (j + step) % nd
        d_copy(step, to, step, to).start()
    red_d[0] = total[pl.ds(pl.multiple_of(j * size, size), size), :]
    for step in range(1, nd):
        d_copy(step, j, step, js).wait_recv()
    here = red_d[0]
    for step in range(1, nd):
        here = here + red_d[step]
    red_c[0] = here

    def c_copy(step):
        return remote(red_c.at[0], red_c.at[step], c_send.at[step], c_recv.at[step], ((i + step) % nz, j))

    for step in range(1, nz):
        c_copy(step).start()
    for step in range(1, nz):
        c_copy(step).wait_recv()
    for step in range(1, nz):
        here = here + red_c[step]
    out[...] = here

    for step in range(1, nz):
        c_copy(step).wait_send()
    for step in range(1, nd):
        d_copy(step, j, step, js).wait_send()
    for n in range(8):
        lg_copy(0, n).wait_send()

    @pl.when(middle)
    def _():
        for n in range(8):
            lg_copy(1, n).wait_send()
        for n in range(AHEAD):
            m_copy(2 * per - AHEAD + n).wait_send()
        for n in range((nz - 1) * per):
            in_copy(n, False).wait_send()

    @pl.when(is_end)
    def _():
        for h in range(halves):
            le_copy(h).wait_send()
        for k in range(per):
            e_copy(k).wait_send()
        te_copy().wait_send()


def shards(nz, nd, main, vectors_left, vectors_right, amplitudes):
    count_a, count_c, left_q = vectors_left.shape
    count_b, count_d, right_q = vectors_right.shape
    pairs = amplitudes.shape[2]
    rest = count_d - main
    per = right_q // CHUNK
    f32, bf16 = jnp.float32, jnp.bfloat16
    columns = count_a * count_c
    dma = pltpu.SemaphoreType.DMA
    hbm = pl.BlockSpec(memory_space=pl.ANY)
    results = pl.pallas_call(
        functools.partial(kernel, nz, nd, main),
        out_shape=[
            jax.ShapeDtypeStruct((pairs // nd, count_a * count_b), f32),
            jax.ShapeDtypeStruct((2, nd, left_q // CHUNK, count_a, CHUNK, count_c), f32),
            jax.ShapeDtypeStruct((nz, per, count_d, count_b, CHUNK), f32),
            jax.ShapeDtypeStruct((count_c, rest, pairs), f32),
        ],
        in_specs=[hbm] * 3,
        out_specs=[pl.BlockSpec(memory_space=pltpu.VMEM), hbm, hbm, hbm],
        scratch_shapes=[
            pltpu.VMEM((count_d * count_b, columns), f32),
            pltpu.VMEM((rest * count_b, columns), f32),
            pltpu.VMEM((count_a, CHUNK, count_c), f32),
            pltpu.VMEM((count_d, count_b, CHUNK), f32),
            pltpu.VMEM((3 * CHUNK, columns), bf16),
            pltpu.VMEM((count_d * count_b, 3 * CHUNK), bf16),
            pltpu.VMEM((2, count_c, 8, pairs), f32),
            pltpu.VMEM((count_a * count_b, pairs), f32),
            pltpu.VMEM((nd, pairs // nd, count_a * count_b), f32),
            pltpu.VMEM((nz, pairs // nd, count_a * count_b), f32),
            dma(((nz - 1) * per,)), dma(((nz - 1) * per,)),
            dma((2 * per,)), dma((2 * per,)),
            dma((per,)), dma((per,)),
            dma((2,)), dma((2,)),
            dma, dma,
            dma((2, 8)), dma((2, 8)),
            dma((nd,)), dma((nd,)),
            dma((nz,)), dma((nz,)),
            dma((3,)), dma((2,)), dma((per,)),
        ],
        compiler_params=pltpu.CompilerParams(
            collective_id=0, has_side_effects=True, vmem_limit_bytes=52 * 2**20),
        name="ladder",
    )(vectors_left, jnp.transpose(vectors_right, (1, 0, 2)), amplitudes)
    whole = results[0].reshape(pairs // nd, count_a, count_b)
    width = count_b // nz
    return lax.dynamic_slice_in_dim(whole, lax.axis_index("vc") * width, width, axis=2)


def solution(mesh):
    nz, nd = mesh.shape["vc"], mesh.shape["vd"]
    fits = nz == 4 and nd == 8
    body = functools.partial(shards, nz, nd, 88) if fits else plain
    return jax.shard_map(
        body,
        mesh=mesh,
        in_specs=(P(None, "vc", "vd"), P(None, "vd", "vc"), P("vc", "vd", None)),
        out_specs=P("vd", None, "vc"),
        check_vma=False,
    )
```

time: 733 us -> 621 us (0.85)
  Pallas kernels: 719 us -> 608 us
    pallas_call x1, Pallas kernels: 719 us -> 608 us  [shards(): pl.pallas_call(functools.partial(kernel, nz, nd, main), out_shape=[jax.Sh...]
where the time goes in v3:
time: 621 us; the launch traced here: 620 us
  Pallas kernels  608 us (98%)
  local copies, waits for them, and re-layouts  12.3 us (2%)
    pallas_call x1, Pallas kernels, shards(): pl.pallas_call(functools.partial(kernel, nz, nd, main), out_shape=[jax.Sh...  608 us

profile of v3, /device:TPU:0, one launch (start us, length us, event | category | flops | bytes accessed | tf_op | source)
XLA Modules:
  0.0 620.2 jit_solution(7304312513106015562)
XLA Ops:
  0.0 11.5 %copy.8 = f32[16,128,1024]{2,0,1:T(8,128)} copy(f32[16,128,1024]{2,1,0:T(8,128)} %param.4) | data formatting | bytes 16777216 | tf_op args[1]
  11.5 608.0 %ladder.1 = (f32[16,128]{1,0:T(8,128)S(1)}, f32[2,8,2,8,256,256]{5,4,3,2,1,0:T(8,128)}, f32[4,4,128,16,256]{4,3,2,1,0:T(8,128)}, f32[256,40,128]{2,1,0:T(8,128)}) custom-call(f32[8,256,512]{2,1,0:T(8,128)} %left.1, f32[128,16,1024]{2,1,0:T(8,128)} %bitcast.4, f32[256,128,128]{2,1,0:T(8,128)} %amps.1), custom_call_target="tpu_custom_call" | custom-call | tf_op jit(solution)/shard_map/ladder/pallas_call | solution.py:456
  619.5 0.1 copy.6
  619.6 0.6 constant_dynamic-slice_fusion

commit v4 on v3

--- a/solution.py
+++ b/solution.py
@@ -160,20 +160,21 @@
             rs[rows, CHUNK:2 * CHUNK] = hi
             rs[rows, 2 * CHUNK:3 * CHUNK] = lo
 
-    def multiply(target, spans):
-        @pl.loop(0, count_a)
+    def multiply(target, span):
+        first, size, wide = span
+        width = wide * count_c
+
+        @pl.loop(0, count_a // wide)
         def _(a):
-            cols = pl.ds(pl.multiple_of(a * count_c, count_c), count_c)
-            for start, first, size in spans:
-                target[pl.ds(start, size), cols] += jnp.dot(
-                    rs[pl.ds(first, size), :], ls[:, cols], preferred_element_type=jnp.float32)
-
-    half = rows_main // 2
-    main_spans = ((0, 0, half), (half, half, half))
-    rest_spans = main_spans + ((rows_main, rows_main, rows_rest),)
-    far_spans = ((0, rows_main, rows_rest),)
-
-    def run(first, last, where, g, parts, target, spans):
+            cols = pl.ds(pl.multiple_of(a * width, width), width)
+            target[0:size, cols] += jnp.dot(
+                rs[pl.ds(first, size), :], ls[:, cols], preferred_element_type=jnp.float32)
+
+    main_span = (0, rows_main, 2)
+    whole_span = (0, rows_main + rows_rest, 2)
+    far_span = (rows_main, rows_rest, 4)
+
+    def run(first, last, where, g, parts, target, span):
         def loads(q):
             block, k = where(q)
             return [load_left(g, block, k)] + [load_right(block, k, *part) for part in parts]
@@ -195,7 +196,7 @@
                 for copy in loads(q + 1):
                     copy.start()
 
-            multiply(target, spans)
+            multiply(target, span)
             return carry
 
         lax.fori_loop(first, last, task, 0)
@@ -298,7 +299,7 @@
             def last(t):
                 return jnp.where(t < 4, 0, jnp.minimum(t + 5, 4 * t - 10))
 
-            run(last(t - 1), last(t), end_task, 0, ((0, main),), acc, main_spans)
+            run(last(t - 1), last(t), end_task, 0, ((0, main),), acc, main_span)
 
     @pl.when(middle)
     def _():
@@ -345,8 +346,8 @@
             def last_far(t):
                 return jnp.where(t < 5, 0, jnp.where(t < 7, 5 * t - 19, 16))
 
-            run(last(t - 1), last(t), middle_task, 0, ((0, main), (main, rest)), acc, rest_spans)
-            run(last_far(t - 1), last_far(t), far_task, 1, ((main, rest),), far, far_spans)
+            run(last(t - 1), last(t), middle_task, 0, ((0, main), (main, rest)), acc, whole_span)
+            run(last_far(t - 1), last_far(t), far_task, 1, ((main, rest),), far, far_span)
 
     total[...] = jnp.zeros_like(total)
 
@@ -496,7 +497,7 @@
 def solution(mesh):
     nz, nd = mesh.shape["vc"], mesh.shape["vd"]
     fits = nz == 4 and nd == 8
-    body = functools.partial(shards, nz, nd, 88) if fits else plain
+    body = functools.partial(shards, nz, nd, 96) if fits else plain
     return jax.shard_map(
         body,
         mesh=mesh,

time: 621 us -> 609 us (0.981)
  Pallas kernels: 608 us -> 596 us
    pallas_call x1, Pallas kernels: 608 us -> 596 us  [shards(): pl.pallas_call(functools.partial(kernel, nz, nd, main), out_shape=[jax.Sh...]
where the time goes in v4:
time: 609 us; the launch traced here: 608 us
  Pallas kernels  596 us (98%)
  local copies, waits for them, and re-layouts  12.3 us (2%)
    pallas_call x1, Pallas kernels, shards(): pl.pallas_call(functools.partial(kernel, nz, nd, main), out_shape=[jax.Sh...  596 us

profile of v4, /device:TPU:0, one launch (start us, length us, event | category | flops | bytes accessed | tf_op | source)
XLA Modules:
  0.0 608.0 jit_solution(6864642536932437198)
XLA Ops:
  0.0 11.5 %copy.8 = f32[16,128,1024]{2,0,1:T(8,128)} copy(f32[16,128,1024]{2,1,0:T(8,128)} %param.4) | data formatting | bytes 16777216 | tf_op args[1]
  11.5 595.7 %ladder.1 = (f32[16,128]{1,0:T(8,128)S(1)}, f32[2,8,2,8,256,256]{5,4,3,2,1,0:T(8,128)}, f32[4,4,128,16,256]{4,3,2,1,0:T(8,128)}, f32[256,32,128]{2,1,0:T(8,128)}) custom-call(f32[8,256,512]{2,1,0:T(8,128)} %left.1, f32[128,16,1024]{2,1,0:T(8,128)} %bitcast.4, f32[256,128,128]{2,1,0:T(8,128)} %amps.1), custom_call_target="tpu_custom_call" | custom-call | tf_op jit(solution)/shard_map/ladder/pallas_call | solution.py:457
  607.3 0.1 copy.6
  607.4 0.6 constant_dynamic-slice_fusion

commit v5 on v4

--- a/solution.py
+++ b/solution.py
@@ -330,24 +330,21 @@
                 lg_first(1)
                 lg_last(0)
 
-            @pl.when(t == 4)
+            @pl.when(t == 5)
             def _():
                 lg_second(1)
 
-            @pl.when(t == 5)
+            @pl.when(t == 6)
             def _():
                 lg_third(1)
-                lg_last(1)
 
             def last(t):
-                late = jnp.where(t < 6, 4 + 2 * t, 9 + t)
-                return jnp.where(t < 2, 0, jnp.where(t == 2, 7, late))
-
-            def last_far(t):
-                return jnp.where(t < 5, 0, jnp.where(t < 7, 5 * t - 19, 16))
+                return jnp.where(t < 2, 0, jnp.minimum(3 * t - 1, 9 + t))
 
             run(last(t - 1), last(t), middle_task, 0, ((0, main), (main, rest)), acc, whole_span)
-            run(last_far(t - 1), last_far(t), far_task, 1, ((main, rest),), far, far_span)
+
+        lg_last(1)
+        run(0, nz * per, far_task, 1, ((main, rest),), far, far_span)
 
     total[...] = jnp.zeros_like(total)
 
@@ -497,7 +494,7 @@
 def solution(mesh):
     nz, nd = mesh.shape["vc"], mesh.shape["vd"]
     fits = nz == 4 and nd == 8
-    body = functools.partial(shards, nz, nd, 96) if fits else plain
+    body = functools.partial(shards, nz, nd, 104) if fits else plain
     return jax.shard_map(
         body,
         mesh=mesh,

time: 609 us -> 620 us (1.018)
  Pallas kernels: 596 us -> 607 us
    pallas_call x1, Pallas kernels: 596 us -> 607 us  [shards(): pl.pallas_call(functools.partial(kernel, nz, nd, main), out_shape=[jax.Sh...]
where the time goes in v5:
time: 620 us; the launch traced here: 619 us
  Pallas kernels  607 us (98%)
  local copies, waits for them, and re-layouts  12.3 us (2%)
    pallas_call x1, Pallas kernels, shards(): pl.pallas_call(functools.partial(kernel, nz, nd, main), out_shape=[jax.Sh...  607 us

profile of v5, /device:TPU:0, one launch (start us, length us, event | category | flops | bytes accessed | tf_op | source)
XLA Modules:
  0.0 619.1 jit_solution(10183514389636013334)
XLA Ops:
  0.0 11.5 %copy.8 = f32[16,128,1024]{2,0,1:T(8,128)} copy(f32[16,128,1024]{2,1,0:T(8,128)} %param.4) | data formatting | bytes 16777216 | tf_op args[1]
  11.5 606.8 %ladder.1 = (f32[16,128]{1,0:T(8,128)S(1)}, f32[2,8,2,8,256,256]{5,4,3,2,1,0:T(8,128)}, f32[4,4,128,16,256]{4,3,2,1,0:T(8,128)}, f32[256,24,128]{2,1,0:T(8,128)}) custom-call(f32[8,256,512]{2,1,0:T(8,128)} %left.1, f32[128,16,1024]{2,1,0:T(8,128)} %bitcast.4, f32[256,128,128]{2,1,0:T(8,128)} %amps.1), custom_call_target="tpu_custom_call" | custom-call | tf_op jit(solution)/shard_map/ladder/pallas_call | solution.py:454
  618.4 0.1 copy.6
  618.5 0.6 constant_dynamic-slice_fusion
